TPU v7x, 32 devices: a whole 2x2x4 slice. The times are simulated.
32 devices in a mesh: grp: 2 (over x), row: 8 (over z, y), col: 2 (over core).
Axes of the slice: x: 2, y: 2, z: 4, core: 2. Of those that a mesh axis runs over, the one named last changes fastest.
Arguments:
- state: float32 [4, 256, 4096], P(None, ('grp', 'row', 'col')), parts along dimension 1, may hold values from -1.5 to 4.5, as said below
- bed_slope: float32 [2, 256, 4096], P(None, ('grp', 'row', 'col')), parts along dimension 1, may hold values from -1.2 to 1.2
- terrain: int32 [256, 4096], P(('grp', 'row', 'col')), parts along dimension 0, may hold values from 0 to 3
- wet_mask: int32 [256, 4096], P(('grp', 'row', 'col')), parts along dimension 0, may hold values 0 or 1
- state_cotangent: float32 [4, 256, 4096], P(None, ('grp', 'row', 'col')), parts along dimension 1, may hold values from -12 to 12
- roughness: float32 [4], replicated, may hold values from 0.5 to 2
- first_weight: float32 [32, 6], replicated, may hold values from -2.5 to 2.5
- second_weight: float32 [32, 32], replicated, may hold values from -1 to 1
- third_weight: float32 [32, 32], replicated, may hold values from -1 to 1
- output_weight: float32 [3, 32], replicated, may hold values from -1 to 1
- biases: float32 [3, 32], replicated, may hold values from -2 to 2
Outputs:
- final_state: float32 [4, 256, 4096], P(None, ('grp', 'row', 'col')), parts along dimension 1
- state_grad: float32 [4, 256, 4096], P(None, ('grp', 'row', 'col')), parts along dimension 1
- first_grad: float32 [64, 6], P('grp'), parts along dimension 0
- second_grad: float32 [64, 32], P('grp'), parts along dimension 0
- third_grad: float32 [64, 32], P('grp'), parts along dimension 0
- output_grad: float32 [6, 32], P('grp'), parts along dimension 0
- bias_grad: float32 [6, 32], P('grp'), parts along dimension 0
There are 2 independent parts, one for each index of `grp`. A program takes and returns all parts, laid end to end along the dimension named above; an argument that names none is the same for every part. Nothing has to cross between parts.
Inputs may be any that keep to these rules, and one draw needn't show every extreme that they name: `state`: depths are positive.
All inputs are finite; a program needn't handle non-finite values. No bound on the sum of `wet_mask` on one device may be relied on, other than what follows from the above.
Results may differ from a plain program's by a relative error of at most 0.00013.
Values sent between devices are 32-bit elements; how exact they have to be, the bound alone decides.
A program may use at most 128 MiB of HBM per device.

v0:
```python
import math

import jax
import jax.numpy as jnp
from jax import lax
from jax.sharding import PartitionSpec as P

STEPS = 6


GRAVITY = 2.0
COURANT = 0.5
SMOOTH = 0.2
EXACT = lax.Precision.HIGHEST


def extended(x, sides, width):
    for axis, dim in sides:
        devices, length = (lax.axis_size(axis), x.shape[dim])
        up = [(i, (i + 1) % devices) for i in range(devices - 1)]
        down = [(j, i) for i, j in up]
        last = lax.slice_in_dim(x, length - width, length, axis=dim)
        initial = lax.slice_in_dim(x, 0, width, axis=dim)
        before = lax.ppermute(last, axis, up)
        after = lax.ppermute(initial, axis, down)
        x = jnp.concatenate([before, x, after], axis=dim)
    return x


def network(features, first_weight, second_weight, third_weight, output_weight, biases):
    hidden = jnp.tanh(
        jnp.dot(first_weight, features, precision=EXACT, preferred_element_type=jnp.float32)
        + biases[0][:, None]
    )
    hidden = jnp.tanh(
        jnp.dot(second_weight, hidden, precision=EXACT, preferred_element_type=jnp.float32)
        + biases[1][:, None]
    )
    hidden = jnp.tanh(
        jnp.dot(third_weight, hidden, precision=EXACT, preferred_element_type=jnp.float32)
        + biases[2][:, None]
    )
    return jnp.dot(output_weight, hidden, precision=EXACT, preferred_element_type=jnp.float32)


def closure(features, weights):
    saved = jax.checkpoint(network)
    mapped = lax.map(lambda row_cells: saved(row_cells, *weights), jnp.moveaxis(features, 1, 0))
    return jnp.moveaxis(mapped, 0, 1)


def cell_roughness(terrain, roughness):
    classes = jnp.arange(roughness.shape[0], dtype=jnp.int32)
    return jnp.sum(
        jnp.where(terrain[None] == classes[:, None, None], roughness[:, None, None], 0.0), axis=0
    )


def update(padded, bed_slope, rough_cell, wet_float, weights, time_step):
    centre = padded[:, 1:-1, 1:-1]
    eastern = padded[:, 1:-1, 2:]
    western = padded[:, 1:-1, :-2]
    northern = padded[:, 2:, 1:-1]
    southern = padded[:, :-2, 1:-1]
    laplace = eastern + western + northern + southern - 4.0 * centre
    along_x = 0.5 * (eastern - western)
    along_y = 0.5 * (northern - southern)
    drag = closure(jnp.concatenate((centre, bed_slope), axis=0), weights)
    depth = centre[0]
    new_depth = depth - time_step * (along_x[1] + along_y[2]) + SMOOTH * laplace[0]
    new_flow_x = (
        centre[1]
        - time_step * GRAVITY * depth * (along_x[0] + bed_slope[0])
        + SMOOTH * laplace[1]
        - time_step * rough_cell * wet_float * drag[0]
    )
    new_flow_y = (
        centre[2]
        - time_step * GRAVITY * depth * (along_y[0] + bed_slope[1])
        + SMOOTH * laplace[2]
        - time_step * rough_cell * wet_float * drag[1]
    )
    new_water = centre[3] + SMOOTH * laplace[3] + time_step * wet_float * drag[2]
    return jnp.stack((new_depth, new_flow_x, new_flow_y, new_water), axis=0)


def shards(
    state,
    bed_slope,
    terrain,
    wet_mask,
    state_cotangent,
    roughness,
    first_weight,
    second_weight,
    third_weight,
    output_weight,
    biases,
):
    rough_cell = cell_roughness(terrain, roughness)
    wet_float = wet_mask.astype(jnp.float32)
    weights = (first_weight, second_weight, third_weight, output_weight, biases)
    pullbacks = []
    current = state
    for number in range(STEPS):
        deepest = lax.pmax(jnp.max(current[0]), ("row", "col"))
        time_step = COURANT / jnp.sqrt(GRAVITY * deepest)
        rimmed = extended(current, ((("row", "col"), 1),), 1)
        padded = jnp.pad(rimmed, ((0, 0), (0, 0), (1, 1)))
        current, pullback = jax.vjp(
            lambda fields, params: update(
                fields, bed_slope, rough_cell, wet_float, params, time_step
            ),
            padded,
            weights,
        )
        pullbacks.append(pullback)
    adjoint = state_cotangent
    summed = jax.tree.map(jnp.zeros_like, weights)
    for number in reversed(range(STEPS)):
        adjoint_pad, partial_grads = pullbacks[number](adjoint)
        partial_grads = lax.psum(
            (
                partial_grads[0],
                partial_grads[1],
                partial_grads[2],
                partial_grads[3],
                partial_grads[4],
            ),
            ("row", "col"),
        )
        summed = jax.tree.map(jnp.add, tuple(summed), tuple(partial_grads))
        interior = adjoint_pad[:, 1:-1, 1:-1]
        rim_rows = jnp.stack((adjoint_pad[:, 0, 1:-1], adjoint_pad[:, -1, 1:-1]), axis=1)
        received = extended(rim_rows, ((("row", "col"), 1),), 1)
        adjoint = interior.at[:, 0, :].add(received[:, 0]).at[:, -1, :].add(received[:, 3])
    cell_count = adjoint.shape[1] * adjoint.shape[2] * lax.axis_size("row") * lax.axis_size("col")
    grad_scale = 1.0 / math.sqrt(cell_count)
    return (
        current,
        adjoint,
        summed[0] * grad_scale,
        summed[1] * grad_scale,
        summed[2] * grad_scale,
        summed[3] * grad_scale,
        summed[4] * grad_scale,
    )


def solution(mesh):
    in_specs = (
        P(None, ("grp", "row", "col"), None),
        P(None, ("grp", "row", "col"), None),
        P(("grp", "row", "col"), None),
        P(("grp", "row", "col"), None),
        P(None, ("grp", "row", "col"), None),
        P(),
        P(),
        P(),
        P(),
        P(),
        P(),
    )
    out_specs = (
        P(None, ("grp", "row", "col"), None),
        P(None, ("grp", "row", "col"), None),
        P("grp", None),
        P("grp", None),
        P("grp", None),
        P("grp", None),
        P("grp", None),
    )
    return jax.shard_map(shards, mesh=mesh, in_specs=in_specs, out_specs=out_specs, check_vma=False)
```

profile of v0, /device:TPU:0, one launch (start us, length us, event | category | flops | bytes accessed | tf_op | source)
XLA Modules:
  0.0 1308.0 jit_solution(6682156056071388093)
XLA Ops:
  9.6 28.8 %while.222 = (s32[]{:T(128)}, f32[8,3,4096]{2,0,1:T(8,128)S(1)}, f32[8,6,4096]{2,1,0:T(8,128)}, f32[32,6]{0,1:T(8,128)S(1)}, f32[32,1]{0,1:T(1,128)S(1)}, /*inde...) while((s32[]{:T(128)}, f32[8,3,4096]{2,0,1:T(8,128)S(1)}, ...), condition=%wide.region_6.7_spmd, body=%wide.region_5.6_spmd.sunk | while | flops 115212288 | bytes 3532921 | solution.py:48
  38.5 36.3 %pmax.42 = f32[]{:T(128)} all-reduce(f32[]{:T(128)} %slice_reduce_fusion), channel_id=1, replica_groups=mesh['grp'=2,'row'=8,'col'=2] {'row','col'}, use_global_device_ids=true, to_apply=%region_1.2 | all-reduce | flops 1 | bytes 8 | tf_op jit(solution)/shard_map/pmax | solution.py:106
  83.3 28.8 %while.223 = (s32[]{:T(128)}, f32[8,3,4096]{2,0,1:T(8,128)S(1)}, f32[8,6,4096]{2,1,0:T(8,128)}, f32[32,6]{0,1:T(8,128)S(1)}, f32[32,1]{0,1:T(1,128)S(1)}, /*inde...) while((s32[]{:T(128)}, f32[8,3,4096]{2,0,1:T(8,128)S(1)}, ...), condition=%wide.region_10.11_spmd, body=%wide.region_9.10_spmd.sunk | while | flops 115212288 | bytes 3532921 | solution.py:48
  112.1 31.2 %pmax.43 = f32[]{:T(128)} all-reduce(f32[]{:T(128)} %get-tuple-element.3096), channel_id=1, replica_groups=mesh['grp'=2,'row'=8,'col'=2] {'row','col'}, use_global_device_ids=true, to_apply=%region_3.4 | all-reduce | flops 1 | bytes 8 | tf_op jit(solution)/shard_map/pmax | solution.py:106
  153.7 28.8 %while.224 = (s32[]{:T(128)}, f32[8,3,4096]{2,0,1:T(8,128)S(1)}, f32[8,6,4096]{2,1,0:T(8,128)}, f32[32,6]{0,1:T(8,128)S(1)}, f32[32,1]{0,1:T(1,128)S(1)}, /*inde...) while((s32[]{:T(128)}, f32[8,3,4096]{2,0,1:T(8,128)S(1)}, ...), condition=%wide.region_14.15_spmd, body=%wide.region_13.14_spmd.sunk | while | flops 115212288 | bytes 3532921 | solution.py:48
  182.5 31.3 %pmax.44 = f32[]{:T(128)} all-reduce(f32[]{:T(128)} %get-tuple-element.3092), channel_id=1, replica_groups=mesh['grp'=2,'row'=8,'col'=2] {'row','col'}, use_global_device_ids=true, to_apply=%region_8.9 | all-reduce | flops 1 | bytes 8 | tf_op jit(solution)/shard_map/pmax | solution.py:106
  222.3 28.8 %while.225 = (s32[]{:T(128)}, f32[8,3,4096]{2,0,1:T(8,128)S(1)}, f32[8,6,4096]{2,1,0:T(8,128)}, f32[32,6]{0,1:T(8,128)S(1)}, f32[32,1]{0,1:T(1,128)S(1)}, /*inde...) while((s32[]{:T(128)}, f32[8,3,4096]{2,0,1:T(8,128)S(1)}, ...), condition=%wide.region_18.19_spmd, body=%wide.region_17.18_spmd.sunk | while | flops 115212288 | bytes 3532921 | solution.py:48
  251.1 31.3 %pmax.45 = f32[]{:T(128)} all-reduce(f32[]{:T(128)} %get-tuple-element.3088), channel_id=1, replica_groups=mesh['grp'=2,'row'=8,'col'=2] {'row','col'}, use_global_device_ids=true, to_apply=%region_12.13 | all-reduce | flops 1 | bytes 8 | tf_op jit(solution)/shard_map/pmax | solution.py:106
  290.9 28.8 %while.226 = (s32[]{:T(128)}, f32[8,3,4096]{2,0,1:T(8,128)S(1)}, f32[8,6,4096]{2,1,0:T(8,128)}, f32[32,6]{0,1:T(8,128)S(1)}, f32[32,1]{0,1:T(1,128)S(1)}, /*inde...) while((s32[]{:T(128)}, f32[8,3,4096]{2,0,1:T(8,128)S(1)}, ...), condition=%wide.region_22.23_spmd, body=%wide.region_21.22_spmd.sunk | while | flops 115212288 | bytes 3532921 | solution.py:48
  319.8 31.3 %pmax.46 = f32[]{:T(128)} all-reduce(f32[]{:T(128)} %get-tuple-element.3084), channel_id=1, replica_groups=mesh['grp'=2,'row'=8,'col'=2] {'row','col'}, use_global_device_ids=true, to_apply=%region_16.17 | all-reduce | flops 1 | bytes 8 | tf_op jit(solution)/shard_map/pmax | solution.py:106
  354.5 30.1 %pmax.47 = f32[]{:T(128)} all-reduce(f32[]{:T(128)} %get-tuple-element.3080), channel_id=1, replica_groups=mesh['grp'=2,'row'=8,'col'=2] {'row','col'}, use_global_device_ids=true, to_apply=%region_20.21 | all-reduce | flops 1 | bytes 8 | tf_op jit(solution)/shard_map/pmax | solution.py:106
  390.9 10.0 collective-permute-start.11
  403.2 28.9 %while.227 = (s32[]{:T(128)}, f32[8,3,4096]{2,0,1:T(8,128)S(1)}, f32[8,6,4096]{2,1,0:T(8,128)}, f32[32,6]{0,1:T(8,128)S(1)}, f32[32,1]{0,1:T(1,128)S(1)}, /*inde...) while((s32[]{:T(128)}, f32[8,3,4096]{2,0,1:T(8,128)S(1)}, ...), condition=%wide.region_24.25_spmd, body=%wide.region_23.24_spmd.sunk | while | flops 115212288 | bytes 3532921 | solution.py:48
  440.7 121.7 %while.228 = (s32[]{:T(128)}, f32[32,6]{0,1:T(8,128)S(1)}, f32[32,32]{1,0:T(8,128)S(1)}, f32[32,32]{1,0:T(8,128)S(1)}, f32[3,32]{1,0:T(4,128)}, /*index=5*/f32[3...) while((s32[]{:T(128)}, f32[32,6]{0,1:T(8,128)S(1)}, ...), condition=%wide.region_29.30_spmd.clone, body=%wide.region_25.29_spmd.clone.sunk | while | flops 342102880 | bytes 15640683 | solution.py:48
  579.2 122.1 %while.229 = (s32[]{:T(128)}, f32[32,6]{0,1:T(8,128)S(1)}, f32[32,32]{1,0:T(8,128)S(1)}, f32[32,32]{1,0:T(8,128)S(1)}, f32[3,32]{1,0:T(4,128)}, /*index=5*/f32[3...) while((s32[]{:T(128)}, f32[32,6]{0,1:T(8,128)S(1)}, ...), condition=%wide.region_34.35_spmd.clone, body=%wide.region_30.34_spmd.clone.sunk | while | flops 342102880 | bytes 15640683 | solution.py:48
  703.5 4.9 collective-permute-start.14
  719.4 122.6 %while.230 = (s32[]{:T(128)}, f32[32,6]{0,1:T(8,128)S(1)}, f32[32,32]{1,0:T(8,128)S(1)}, f32[32,32]{1,0:T(8,128)S(1)}, f32[3,32]{1,0:T(4,128)}, /*index=5*/f32[3...) while((s32[]{:T(128)}, f32[32,6]{0,1:T(8,128)S(1)}, ...), condition=%wide.region_39.40_spmd.clone, body=%wide.region_35.39_spmd.clone.sunk | while | flops 342102880 | bytes 15640683 | solution.py:48
  844.1 4.3 collective-permute-start.16
  859.5 121.7 %while.231 = (s32[]{:T(128)}, f32[32,6]{0,1:T(8,128)S(1)}, f32[32,32]{1,0:T(8,128)S(1)}, f32[32,32]{1,0:T(8,128)S(1)}, f32[3,32]{1,0:T(4,128)}, /*index=5*/f32[3...) while((s32[]{:T(128)}, f32[32,6]{0,1:T(8,128)S(1)}, ...), condition=%wide.region_44.45_spmd.clone, body=%wide.region_40.44_spmd.clone.sunk | while | flops 342102880 | bytes 15640683 | solution.py:48
  983.4 4.4 collective-permute-start.18
  998.7 121.8 %while.232 = (s32[]{:T(128)}, f32[32,6]{0,1:T(8,128)S(1)}, f32[32,32]{1,0:T(8,128)S(1)}, f32[32,32]{1,0:T(8,128)S(1)}, f32[3,32]{1,0:T(4,128)}, /*index=5*/f32[3...) while((s32[]{:T(128)}, f32[32,6]{0,1:T(8,128)S(1)}, ...), condition=%wide.region_49.50_spmd.clone, body=%wide.region_45.49_spmd.clone.sunk | while | flops 342102880 | bytes 15640683 | solution.py:48
  1122.7 4.4 collective-permute-start.20
  1136.9 94.3 %while.233 = (s32[]{:T(128)}, f32[32,6]{0,1:T(8,128)S(1)}, f32[32,32]{1,0:T(8,128)S(1)}, f32[32,32]{1,0:T(8,128)}, f32[3,32]{1,0:T(4,128)}, /*index=5*/f32[3,32]...) while((s32[]{:T(128)}, f32[32,6]{0,1:T(8,128)S(1)}, ...), condition=%wide.region_54.55_spmd.clone, body=%wide.region_50.54_spmd.clone.sunk | while | flops 342102880 | bytes 14890147 | solution.py:48
  1142.7 3.1 dynamic_update_slice.103
  1154.5 3.1 dynamic_update_slice.103
  1166.3 3.1 dynamic_update_slice.103
  1178.1 3.1 dynamic_update_slice.103
  1189.9 3.1 dynamic_update_slice.103
  1201.7 3.1 dynamic_update_slice.103
  1213.5 3.1 dynamic_update_slice.103
  1225.3 3.1 dynamic_update_slice.103
  1237.3 60.1 %all-reduce.144 = (f32[32,6]{0,1:T(8,128)S(1)}, f32[32,32]{1,0:T(8,128)S(1)}, f32[32,32]{1,0:T(8,128)S(1)}, f32[3,32]{1,0:T(4,128)S(1)}, f32[3,32]{1,0:T(4,128)S(1)}) all-reduce(f32[32,6]{0,1:T(8,128)S(1)} %add_add_fusion.8, f32[32,32]{1,0:T(8,128)S(1)} %get-tuple-element.3309, ...), channel_id=1, replica_groups=mesh['grp'=2,'row'=8,'col'=2] {'row','col'}, use_global_device_ids=true, to_apply=%region_55.56 | all-reduce | flops 2432 | bytes 19456 | tf_op jit(solution)/shard_map/psum | solution.py:122
  (2372 shorter events, 985.2 us)
Async XLA Ops:
  2.1 73.4 %collective-permute-start = (f32[4,1,4096]{2,1,0:T(1,128)S(1)}, f32[4,1,4096]{2,1,0:T(1,128)S(1)}, u32[]{:S(2)}, u32[]{:S(2)}) collective-permute-start(f32[4,1,4096]{2,1,0:T(1,128)S(1)} %get-tuple-element.3299), channel_id=1, source_target_pairs={{0,1},{1,2},{2,3},{3,4},{4,5},{5,6},{6,7},{7,8},{8,9},{9,10},{10,1... | collective-permute-start | bytes 196616 | tf_op jit(solution)/shard_map/ppermute | solution.py:24
  4.5 71.1 %collective-permute-start.1 = (f32[4,1,4096]{2,1,0:T(1,128)S(1)}, f32[4,1,4096]{2,1,0:T(1,128)S(1)}, u32[]{:S(2)}, u32[]{:S(2)}) collective-permute-start(f32[4,1,4096]{2,1,0:T(1,128)S(1)} %get-tuple-element.3300), channel_id=1, source_target_pairs={{1,0},{2,1},{3,2},{4,3},{5,4},{6,5},{7,6},{8,7},{9,8},{10,9},{11,1... | collective-permute-start | bytes 196616 | tf_op jit(solution)/shard_map/ppermute | solution.py:25
  9.6 65.8 %copy-start.194 = (s32[8,4096]{1,0:T(8,128)S(1)}, s32[8,4096]{1,0:T(8,128)}, u32[]{:S(2)}) copy-start(s32[8,4096]{1,0:T(8,128)} %param.61) | copy-start | bytes 393220
  9.6 65.8 %copy-start.221 = (f32[4]{0:T(128)S(1)}, f32[4]{0:T(128)}, u32[]{:S(2)}) copy-start(f32[4]{0:T(128)} %param.64) | copy-start | bytes 52
  38.4 37.1 %copy-start.162 = (f32[32,1]{0,1:T(1,128)}, f32[32,1]{0,1:T(1,128)S(1)}, u32[]{:S(2)}) copy-start(f32[32,1]{0,1:T(1,128)S(1)} %get-tuple-element.4966) | copy-start | bytes 388
  38.5 37.1 %copy-start.170 = (f32[32,1]{0,1:T(1,128)}, f32[32,1]{0,1:T(1,128)S(1)}, u32[]{:S(2)}) copy-start(f32[32,1]{0,1:T(1,128)S(1)} %get-tuple-element.4971) | copy-start | bytes 388
  77.5 70.4 %copy-start.21 = (f32[1,8,4096]{2,1,0:T(8,128)}, f32[1,8,4096]{2,1,0:T(8,128)S(1)}, u32[]{:S(2)}) copy-start(f32[1,8,4096]{2,1,0:T(8,128)S(1)} %get-tuple-element.3097) | copy-start | bytes 393220
  78.5 65.5 %collective-permute-start.2 = (f32[4,1,4096]{2,1,0:T(1,128)S(1)}, f32[4,1,4096]{2,1,0:T(1,128)S(1)}, u32[]{:S(2)}, u32[]{:S(2)}) collective-permute-start(f32[4,1,4096]{2,1,0:T(1,128)S(1)} %get-tuple-element.3297), channel_id=1, source_target_pairs={{0,1},{1,2},{2,3},{3,4},{4,5},{5,6},{6,7},{7,8},{8,9},{9,10},{10,1... | collective-permute-start | bytes 196616 | tf_op jit(solution)/shard_map/ppermute | solution.py:24
  79.8 64.2 %collective-permute-start.3 = (f32[4,1,4096]{2,1,0:T(1,128)S(1)}, f32[4,1,4096]{2,1,0:T(1,128)S(1)}, u32[]{:S(2)}, u32[]{:S(2)}) collective-permute-start(f32[4,1,4096]{2,1,0:T(1,128)S(1)} %get-tuple-element.3298), channel_id=1, source_target_pairs={{1,0},{2,1},{3,2},{4,3},{5,4},{6,5},{7,6},{8,7},{9,8},{10,9},{11,1... | collective-permute-start | bytes 196616 | tf_op jit(solution)/shard_map/ppermute | solution.py:25
  147.6 69.0 %copy-start.23 = (f32[1,8,4096]{2,1,0:T(8,128)}, f32[1,8,4096]{2,1,0:T(8,128)S(1)}, u32[]{:S(2)}) copy-start(f32[1,8,4096]{2,1,0:T(8,128)S(1)} %get-tuple-element.3093) | copy-start | bytes 393220
  148.6 65.9 %collective-permute-start.4 = (f32[4,1,4096]{2,1,0:T(1,128)S(1)}, f32[4,1,4096]{2,1,0:T(1,128)S(1)}, u32[]{:S(2)}, u32[]{:S(2)}) collective-permute-start(f32[4,1,4096]{2,1,0:T(1,128)S(1)} %get-tuple-element.3295), channel_id=1, source_target_pairs={{0,1},{1,2},{2,3},{3,4},{4,5},{5,6},{6,7},{7,8},{8,9},{9,10},{10,1... | collective-permute-start | bytes 196616 | tf_op jit(solution)/shard_map/ppermute | solution.py:24
  149.9 64.6 %collective-permute-start.5 = (f32[4,1,4096]{2,1,0:T(1,128)S(1)}, f32[4,1,4096]{2,1,0:T(1,128)S(1)}, u32[]{:S(2)}, u32[]{:S(2)}) collective-permute-start(f32[4,1,4096]{2,1,0:T(1,128)S(1)} %get-tuple-element.3296), channel_id=1, source_target_pairs={{1,0},{2,1},{3,2},{4,3},{5,4},{6,5},{7,6},{8,7},{9,8},{10,9},{11,1... | collective-permute-start | bytes 196616 | tf_op jit(solution)/shard_map/ppermute | solution.py:25
  216.6 68.7 %copy-start.25 = (f32[1,8,4096]{2,1,0:T(8,128)}, f32[1,8,4096]{2,1,0:T(8,128)S(1)}, u32[]{:S(2)}) copy-start(f32[1,8,4096]{2,1,0:T(8,128)S(1)} %get-tuple-element.3089) | copy-start | bytes 393220
  217.4 65.7 %collective-permute-start.6 = (f32[4,1,4096]{2,1,0:T(1,128)S(1)}, f32[4,1,4096]{2,1,0:T(1,128)S(1)}, u32[]{:S(2)}, u32[]{:S(2)}) collective-permute-start(f32[4,1,4096]{2,1,0:T(1,128)S(1)} %get-tuple-element.3293), channel_id=1, source_target_pairs={{0,1},{1,2},{2,3},{3,4},{4,5},{5,6},{6,7},{7,8},{8,9},{9,10},{10,1... | collective-permute-start | bytes 196616 | tf_op jit(solution)/shard_map/ppermute | solution.py:24
  218.8 64.4 %collective-permute-start.7 = (f32[4,1,4096]{2,1,0:T(1,128)S(1)}, f32[4,1,4096]{2,1,0:T(1,128)S(1)}, u32[]{:S(2)}, u32[]{:S(2)}) collective-permute-start(f32[4,1,4096]{2,1,0:T(1,128)S(1)} %get-tuple-element.3294), channel_id=1, source_target_pairs={{1,0},{2,1},{3,2},{4,3},{5,4},{6,5},{7,6},{8,7},{9,8},{10,9},{11,1... | collective-permute-start | bytes 196616 | tf_op jit(solution)/shard_map/ppermute | solution.py:25
  285.1 102.2 %copy-start.27 = (f32[1,8,4096]{2,1,0:T(8,128)}, f32[1,8,4096]{2,1,0:T(8,128)S(1)}, u32[]{:S(2)}) copy-start(f32[1,8,4096]{2,1,0:T(8,128)S(1)} %get-tuple-element.3085) | copy-start | bytes 393220
  286.1 65.7 %collective-permute-start.8 = (f32[4,1,4096]{2,1,0:T(1,128)S(1)}, f32[4,1,4096]{2,1,0:T(1,128)S(1)}, u32[]{:S(2)}, u32[]{:S(2)}) collective-permute-start(f32[4,1,4096]{2,1,0:T(1,128)S(1)} %get-tuple-element.3291), channel_id=1, source_target_pairs={{0,1},{1,2},{2,3},{3,4},{4,5},{5,6},{6,7},{7,8},{8,9},{9,10},{10,1... | collective-permute-start | bytes 196616 | tf_op jit(solution)/shard_map/ppermute | solution.py:24
  287.4 64.4 %collective-permute-start.9 = (f32[4,1,4096]{2,1,0:T(1,128)S(1)}, f32[4,1,4096]{2,1,0:T(1,128)S(1)}, u32[]{:S(2)}, u32[]{:S(2)}) collective-permute-start(f32[4,1,4096]{2,1,0:T(1,128)S(1)} %get-tuple-element.3292), channel_id=1, source_target_pairs={{1,0},{2,1},{3,2},{4,3},{5,4},{6,5},{7,6},{8,7},{9,8},{10,9},{11,1... | collective-permute-start | bytes 196616 | tf_op jit(solution)/shard_map/ppermute | solution.py:25
  389.1 43.8 %collective-permute-start.10 = (f32[4,1,4096]{2,1,0:T(1,128)S(1)}, f32[4,1,4096]{2,1,0:T(1,128)S(1)}, u32[]{:S(2)}, u32[]{:S(2)}) collective-permute-start(f32[4,1,4096]{2,1,0:T(1,128)S(1)} %get-tuple-element.3289), channel_id=1, source_target_pairs={{0,1},{1,2},{2,3},{3,4},{4,5},{5,6},{6,7},{7,8},{8,9},{9,10},{10,1... | collective-permute-start | bytes 196616 | tf_op jit(solution)/shard_map/ppermute | solution.py:24
  390.9 42.0 %collective-permute-start.11 = (f32[4,1,4096]{2,1,0:T(1,128)S(1)}, f32[4,1,4096]{2,1,0:T(1,128)S(1)}, u32[]{:S(2)}, u32[]{:S(2)}) collective-permute-start(f32[4,1,4096]{2,1,0:T(1,128)S(1)} %get-tuple-element.3290), channel_id=1, source_target_pairs={{1,0},{2,1},{3,2},{4,3},{5,4},{6,5},{7,6},{8,7},{9,8},{10,9},{11,1... | collective-permute-start | bytes 196616 | tf_op jit(solution)/shard_map/ppermute | solution.py:25
  565.7 5.7 collective-permute-start.12
  568.8 4.1 collective-permute-start.13
  703.5 8.0 collective-permute-start.14
  709.7 3.3 collective-permute-start.15
  844.1 7.2 collective-permute-start.16
  849.8 3.3 collective-permute-start.17
  983.4 7.3 collective-permute-start.18
  989.0 3.3 collective-permute-start.19
  1122.7 7.3 collective-permute-start.20
  1128.4 3.3 collective-permute-start.21
  1299.8 4.6 collective-permute-start.22
  1303.1 3.1 collective-permute-start.23
  (480 other events, 963.7 us)
where the time goes:
time: 1320 us; the launch traced here: 1310 us
  matrix products  536 us (41%)
  local copies, waits for them, and re-layouts  316 us (24%)
  blocking collectives  252 us (19%)
  other arithmetic  122 us (9%)
  starting transfers between devices  57.8 us (4%)
    dynamic_update_slice x192, local copies, waits for them, and re-layouts, closure(): lax.map(lambda row_cells: saved(row_cells, *weights), jnp.moveaxis(featur...  197 us
    pmax x6, blocking collectives, shards(): deepest = lax.pmax(jnp.max(current[0]), ('row', 'col'))  192 us
    dot_general x192, matrix products, network(): jnp.dot(first_weight, features, precision=EXACT, preferred_element_type=j...  148 us
    dot_general x192, matrix products, network(): jnp.dot(second_weight, hidden, precision=EXACT, preferred_element_type=jn...  143 us
    dot_general x192, matrix products, network(): jnp.dot(third_weight, hidden, precision=EXACT, preferred_element_type=jnp...  142 us
    dot_general x144, matrix products, network(): jnp.dot(output_weight, hidden, precision=EXACT, preferred_element_type=jn...  104 us
    psum x1, blocking collectives, shards(): lax.psum((partial_grads[0], partial_grads[1], partial_grads[2], partial_g...  60.1 us
    add_any x48, other arithmetic, closure(): saved(row_cells, *weights)  50.9 us
  transfers between devices with their start and end apart: 24, of which 6 were waited for; matrix products, arithmetic and copies ran while one was open for 15% of the time, Pallas kernels for 0%

commit v1 on v0

v1 whole, which is shorter than its diff:
```python
import functools
import math

import jax
import jax.numpy as jnp
from jax import lax
from jax.experimental import pallas as pl
from jax.experimental.pallas import tpu as pltpu
from jax.sharding import PartitionSpec as P

STEPS = 6
GRAVITY = 2.0
COURANT = 0.5
SMOOTH = 0.2
HID = 32
ROWS = 8
WIDE = HID * ROWS
CHUNK = 512
F32, BF16 = jnp.float32, jnp.bfloat16


def dot(a, b, ca=1, cb=0):
    return lax.dot_general(a, b, (((ca,), (cb,)), ((), ())), preferred_element_type=F32)


def split(x):
    hi = x.astype(BF16)
    lo = (x - hi.astype(F32)).astype(BF16)
    return hi, lo


def split3(x):
    hi = x.astype(BF16)
    rest = x - hi.astype(F32)
    mid = rest.astype(BF16)
    return hi, mid, (rest - mid.astype(F32)).astype(BF16)


def iota(shape, dim):
    return lax.broadcasted_iota(jnp.int32, shape, dim)


def wrapped(index, period):
    return index - period * (index >= period) - period * (index >= 2 * period)


def spread(count, period, transposed=False):
    shape = (HID, count) if transposed else (count, HID)
    stacked, unit = (1, 0) if transposed else (0, 1)
    return ((wrapped(iota(shape, stacked), period) >> 3) == iota(shape, unit)).astype(F32).astype(BF16)


def same_row(shape):
    return (iota(shape, 0) & 7) == (iota(shape, 1) & 7)


def widened(small, rows, cols, transposed, period):
    keep = same_row((rows, cols))
    left, right = spread(rows, rows), spread(cols, period)
    result = []
    for part in split(small):
        half = dot(left, part, 1, 1 if transposed else 0).astype(BF16)
        full = dot(half, right, 1, 1)
        result.append(jnp.where(keep, full, 0.0))
    return result


def stacked3(small, rows, unit, transposed):
    hi, lo = widened(small, rows, 3 * unit, transposed, unit)
    col = iota(hi.shape, 1)
    return jnp.where((col >= unit) & (col < 2 * unit), lo, hi).astype(BF16)


def shifted(x, before, after):
    row, col = iota(x.shape, 0), iota(x.shape, 1)
    length = x.shape[1]
    north = jnp.where(row == ROWS - 1, after, pltpu.roll(x, ROWS - 1, 0))
    south = jnp.where(row == 0, before, pltpu.roll(x, 1, 0))
    east = jnp.where(col == length - 1, 0.0, pltpu.roll(x, length - 1, 1))
    west = jnp.where(col == 0, 0.0, pltpu.roll(x, 1, 1))
    return east, west, north, south


def kernel(
    n, ncol, cols,
    state, bed, terrain, wet_mask, cotangent, params, roughness,
    final, adjoint, grads,
    traj, lam, drag, dfeat, rough_wet, wet, steps_dt,
    w1, w2, w3, w4, w2t, w3t, w4t, w1t, bias,
    g1, g2, g3, g4, gb,
    edge_f, halo_f, edge_b, halo_b, peak, peaks, own_grad, all_grads,
    edge_ss, edge_rs, peak_ss, peak_rs, grad_ss, grad_rs,
):
    me = lax.axis_index("row") * ncol + lax.axis_index("col")

    def device(p):
        return {"row": p // ncol, "col": p % ncol}

    def peer(i):
        return lax.rem(me + i, n)

    before_id, after_id = peer(n - 1), peer(1)
    barrier = pltpu.get_barrier_semaphore()

    @pl.loop(1, n)
    def _(i):
        pl.semaphore_signal(barrier, inc=1, device_id=device(peer(i)), device_id_type=pl.DeviceIdType.MESH)

    m1, m2, m3, m4 = (params[32 * i : 32 * i + 32, :] for i in range(4))
    w1[...] = stacked3(m1, WIDE, 48, False)
    w4t[...] = stacked3(m4, WIDE, 32, True)
    for ref, small, rows, transposed in (
        (w2, m2, WIDE, False), (w3, m3, WIDE, False), (w4, m4, 32, False),
        (w2t, m2, WIDE, True), (w3t, m3, WIDE, True), (w1t, m1, 32, True),
    ):
        for k, part in enumerate(widened(small, rows, WIDE, transposed, WIDE)):
            ref[k] = part.astype(BF16)
    for layer in range(3):
        line = jnp.broadcast_to(params[128 + layer : 129 + layer, :], (128, HID))
        bias[layer] = sum(dot(spread(WIDE, WIDE), part, 1, 1) for part in split3(line))
    for ref in (g1, g2, g3, g4, gb):
        ref[...] = jnp.zeros_like(ref)
    kinds = terrain[...]
    rough = jnp.zeros(kinds.shape, F32)
    for k in range(roughness.shape[0]):
        rough = jnp.where(kinds == k, roughness[k], rough)
    wet[...] = wet_mask[...].astype(F32)
    rough_wet[...] = rough * wet[...]
    traj[0] = state[...]
    lam[...] = cotangent[...]

    pl.semaphore_wait(barrier, n - 1)

    def edge_copies(number, step, edge, halo):
        return [
            pltpu.make_async_remote_copy(
                src_ref=edge.at[step, side], dst_ref=halo.at[step, 1 - side],
                send_sem=edge_ss.at[number, side], recv_sem=edge_rs.at[number, 1 - side],
                device_id=device(target), device_id_type=pl.DeviceIdType.MESH,
            )
            for side, target in ((0, before_id), (1, after_id))
        ]

    def arriving(number, step, edge, halo):
        return [
            pltpu.make_async_remote_copy(
                src_ref=edge.at[step, 1 - side], dst_ref=halo.at[step, side],
                send_sem=edge_ss.at[number, 1 - side], recv_sem=edge_rs.at[number, side],
                device_id=device(before_id), device_id_type=pl.DeviceIdType.MESH,
            )
            for side in (0, 1)
        ]

    def send_edges(number, step, edge, halo, field):
        for f in range(4):
            edge[step, 0, f : f + 1, :] = field(f, 0)
            edge[step, 1, f : f + 1, :] = field(f, ROWS - 1)
        for copy in edge_copies(number, step, edge, halo):
            copy.start()

    def take_edges(number, step, edge, halo):
        for copy in arriving(number, step, edge, halo):
            copy.wait_recv()
        for copy in edge_copies(number, step, edge, halo):
            copy.wait_send()

    def peak_copy(step, i):
        return pltpu.make_async_remote_copy(
            src_ref=peak.at[step], dst_ref=peaks.at[step, me],
            send_sem=peak_ss.at[i], recv_sem=peak_rs.at[step, me],
            device_id=device(peer(i)), device_id_type=pl.DeviceIdType.MESH,
        )

    def peak_arrival(step, i):
        return pltpu.make_async_remote_copy(
            src_ref=peak.at[step], dst_ref=peaks.at[step, peer(i)],
            send_sem=peak_ss.at[i], recv_sem=peak_rs.at[step, peer(i)],
            device_id=device(peer(i)), device_id_type=pl.DeviceIdType.MESH,
        )

    has_before = jnp.where(me > 0, 1.0, 0.0).astype(F32)
    has_after = jnp.where(me < n - 1, 1.0, 0.0).astype(F32)

    def across(tile, width):
        return jnp.concatenate([tile] * (width // 128), axis=1)

    def layer(weight, hi, lo):
        return dot(weight[0], hi) + dot(weight[0], lo) + dot(weight[1], hi)

    def hidden(step, at):
        x = jnp.concatenate([traj[step, :, at], bed[:, at]], axis=0)
        xhi, xlo = split(x)
        a1 = jnp.tanh(dot(w1[...], jnp.concatenate([xhi, xhi, xlo], axis=0)) + across(bias[0], CHUNK))
        s1 = split(a1)
        a2 = jnp.tanh(layer(w2, *s1) + across(bias[1], CHUNK))
        s2 = split(a2)
        a3 = jnp.tanh(layer(w3, *s2) + across(bias[2], CHUNK))
        return (xhi, xlo), a1, s1, a2, s2, a3, split(a3)

    def forward(step, _):
        send_edges(step, step, edge_f, halo_f, lambda f, r: traj[step, 8 * f + r : 8 * f + r + 1, :])
        depth = traj[step, 0:ROWS, :]
        deepest = depth[:, 0:128]
        for k in range(1, cols // 128):
            deepest = jnp.maximum(deepest, depth[:, 128 * k : 128 * k + 128])
        peak[step] = deepest
        peaks[step, me] = deepest

        @pl.loop(1, n)
        def _(i):
            peak_copy(step, i).start()

        @pl.loop(0, cols // CHUNK)
        def _(c):
            at = pl.ds(pl.multiple_of(c * CHUNK, CHUNK), CHUNK)
            s3 = hidden(step, at)[-1]
            drag[:, at] = layer(w4, *s3)

        @pl.loop(1, n)
        def _(i):
            peak_arrival(step, i).wait_recv()
            peak_copy(step, i).wait_send()

        largest = jnp.max(jnp.max(peaks[step], axis=0))
        tile = COURANT / jnp.sqrt(GRAVITY * jnp.full((ROWS, 128), largest, F32))
        steps_dt[step] = tile
        dt = across(tile, cols)
        take_edges(step, step, edge_f, halo_f)
        fields = [traj[step, 8 * f : 8 * f + 8, :] for f in range(4)]
        near = [
            shifted(
                fields[f],
                halo_f[step, 0, f : f + 1, :] * has_before,
                halo_f[step, 1, f : f + 1, :] * has_after,
            )
            for f in range(4)
        ]
        smooth = [SMOOTH * (e + w + n_ + s - 4.0 * fields[f]) for f, (e, w, n_, s) in enumerate(near)]

        def ddx(f):
            return 0.5 * (near[f][0] - near[f][1])

        def ddy(f):
            return 0.5 * (near[f][2] - near[f][3])

        depth = fields[0]
        traj[step + 1, 0:8, :] = depth - dt * (ddx(1) + ddy(2)) + smooth[0]
        traj[step + 1, 8:16, :] = (
            fields[1] - dt * GRAVITY * depth * (ddx(0) + bed[0:8, :]) + smooth[1] - dt * rough_wet[...] * drag[0:8, :]
        )
        traj[step + 1, 16:24, :] = (
            fields[2] - dt * GRAVITY * depth * (ddy(0) + bed[8:16, :]) + smooth[2] - dt * rough_wet[...] * drag[8:16, :]
        )
        traj[step + 1, 24:32, :] = fields[3] + smooth[3] + dt * wet[...] * drag[16:24, :]
        return 0

    lax.fori_loop(0, STEPS, forward, 0)
    final[...] = traj[STEPS]

    def backward(back, _):
        step = STEPS - 1 - back
        number = STEPS + step
        send_edges(number, step, edge_b, halo_b, lambda f, r: lam[8 * f + r : 8 * f + r + 1, :])
        tile = steps_dt[step]

        @pl.loop(0, cols // CHUNK)
        def _(c):
            at = pl.ds(pl.multiple_of(c * CHUNK, CHUNK), CHUNK)
            dt = across(tile, CHUNK)
            pull = -dt * rough_wet[:, at]
            g = jnp.concatenate(
                [pull * lam[8:16, at], pull * lam[16:24, at], dt * wet[:, at] * lam[24:32, at], jnp.zeros((8, CHUNK), F32)],
                axis=0,
            )
            ghi, glo = split(g)
            (xhi, xlo), a1, s1, a2, s2, a3, s3 = hidden(step, at)
            d3 = dot(w4t[...], jnp.concatenate([ghi, ghi, glo], axis=0)) * (1.0 - a3 * a3)
            t3 = split(d3)
            d2 = layer(w3t, *t3) * (1.0 - a2 * a2)
            t2 = split(d2)
            d1 = layer(w2t, *t2) * (1.0 - a1 * a1)
            t1 = split(d1)
            dfeat[:, at] = layer(w1t, *t1)
            both_g = jnp.concatenate([ghi, glo], axis=0)
            both_x = jnp.concatenate([xhi, xlo], axis=0)
            g4[...] += dot(both_g, s3[0], 1, 1) + dot(both_g, s3[1], 1, 1)
            g3[...] += dot(t3[0], s2[0], 1, 1) + dot(t3[0], s2[1], 1, 1) + dot(t3[1], s2[0], 1, 1)
            g2[...] += dot(t2[0], s1[0], 1, 1) + dot(t2[0], s1[1], 1, 1) + dot(t2[1], s1[0], 1, 1)
            g1[...] += dot(t1[0], both_x, 1, 1) + dot(t1[1], both_x, 1, 1)
            for k, d in enumerate((d1, d2, d3)):
                total = d[:, 0:128]
                for j in range(1, CHUNK // 128):
                    total = total + d[:, 128 * j : 128 * j + 128]
                gb[k] += total

        dt = across(tile, cols)
        take_edges(number, step, edge_b, halo_b)
        lams = [lam[8 * f : 8 * f + 8, :] for f in range(4)]
        above = [halo_b[step, 0, f : f + 1, :] * has_before for f in range(4)]
        below = [halo_b[step, 1, f : f + 1, :] * has_after for f in range(4)]
        near = [shifted(lams[f], above[f], below[f]) for f in range(4)]
        smooth = [SMOOTH * (e + w + n_ + s - 4.0 * lams[f]) for f, (e, w, n_, s) in enumerate(near)]
        depth = traj[step, 0:8, :]
        depth_above = halo_f[step, 0, 0:1, :] * has_before
        depth_below = halo_f[step, 1, 0:1, :] * has_after
        e, w, n_, s = shifted(depth, depth_above, depth_below)
        slope_x = 0.5 * (e - w) + bed[0:8, :]
        slope_y = 0.5 * (n_ - s) + bed[8:16, :]
        px_e, px_w, _, _ = shifted(depth * lams[1], depth_above, depth_below)
        _, _, py_n, py_s = shifted(depth * lams[2], depth_above * above[2], depth_below * below[2])
        push = 0.5 * (px_e - px_w + py_n - py_s) - slope_x * lams[1] - slope_y * lams[2]
        lam[0:8, :] = lams[0] + smooth[0] + dt * GRAVITY * push + dfeat[0:8, :]
        lam[8:16, :] = lams[1] + smooth[1] + dt * 0.5 * (near[0][0] - near[0][1]) + dfeat[8:16, :]
        lam[16:24, :] = lams[2] + smooth[2] + dt * 0.5 * (near[0][2] - near[0][3]) + dfeat[16:24, :]
        lam[24:32, :] = lams[3] + smooth[3] + dfeat[24:32, :]
        return 0

    lax.fori_loop(0, STEPS, backward, 0)
    adjoint[...] = lam[...]

    def place(count, period, offset):
        shape = (count, 128)
        return ((wrapped(iota(shape, 0), period) >> 3) + offset == iota(shape, 1)).astype(F32).astype(BF16)

    def collapsed(total, period, col_period, offset):
        rows, width = total.shape
        total = jnp.where(same_row(total.shape), total, 0.0)
        gather = spread(rows, period, transposed=True)
        half = sum(dot(gather, part) for part in split3(total))
        put = place(width, col_period, offset)
        return sum(dot(part, put) for part in split3(half))

    packed = collapsed(g1[...], WIDE, 48, 0)
    packed += collapsed(g2[...], WIDE, WIDE, 32)
    packed += collapsed(g3[...], WIDE, WIDE, 64)
    packed += collapsed(g4[...], 32, WIDE, 96)
    for k in range(3):
        pick = (iota((HID, 128), 0) == 8 + k).astype(F32).astype(BF16)
        half = sum(dot(pick, part, 1, 1) for part in split3(gb[k]))
        packed += sum(dot(part, place(WIDE, WIDE, 96)) for part in split3(half))
    own_grad[...] = packed
    all_grads[me] = packed

    def grad_copy(i):
        return pltpu.make_async_remote_copy(
            src_ref=own_grad, dst_ref=all_grads.at[me],
            send_sem=grad_ss.at[i], recv_sem=grad_rs.at[me],
            device_id=device(peer(i)), device_id_type=pl.DeviceIdType.MESH,
        )

    def grad_arrival(i):
        return pltpu.make_async_remote_copy(
            src_ref=own_grad, dst_ref=all_grads.at[peer(i)],
            send_sem=grad_ss.at[i], recv_sem=grad_rs.at[peer(i)],
            device_id=device(peer(i)), device_id_type=pl.DeviceIdType.MESH,
        )

    @pl.loop(1, n)
    def _(i):
        grad_copy(i).start()

    @pl.loop(1, n)
    def _(i):
        grad_arrival(i).wait_recv()
        grad_copy(i).wait_send()

    grads[...] = jnp.sum(all_grads[...], axis=0) * (1.0 / math.sqrt(ROWS * cols * n))


def shards(
    state, bed_slope, terrain, wet_mask, state_cotangent, roughness,
    first_weight, second_weight, third_weight, output_weight, biases,
):
    nrow, ncol = lax.axis_size("row"), lax.axis_size("col")
    n = nrow * ncol
    cols = state.shape[2]
    assert state.shape[1] == ROWS
    params = jnp.concatenate(
        [
            jnp.pad(first_weight, ((0, 0), (0, HID - first_weight.shape[1]))),
            second_weight,
            third_weight,
            jnp.pad(output_weight, ((0, HID - output_weight.shape[0]), (0, 0))),
            jnp.pad(biases, ((0, 8 - biases.shape[0]), (0, 0))),
        ],
        axis=0,
    )
    vmem = pl.BlockSpec(memory_space=pltpu.VMEM)
    big = (2, WIDE, WIDE)
    final, adjoint, grads = pl.pallas_call(
        functools.partial(kernel, n, ncol, cols),
        out_shape=(
            jax.ShapeDtypeStruct((4 * ROWS, cols), F32),
            jax.ShapeDtypeStruct((4 * ROWS, cols), F32),
            jax.ShapeDtypeStruct((HID, 128), F32),
        ),
        in_specs=[vmem] * 6 + [pl.BlockSpec(memory_space=pltpu.SMEM)],
        out_specs=(vmem, vmem, vmem),
        scratch_shapes=[
            pltpu.VMEM((STEPS + 1, 4 * ROWS, cols), F32),
            pltpu.VMEM((4 * ROWS, cols), F32),
            pltpu.VMEM((4 * ROWS, cols), F32),
            pltpu.VMEM((4 * ROWS, cols), F32),
            pltpu.VMEM((ROWS, cols), F32),
            pltpu.VMEM((ROWS, cols), F32),
            pltpu.VMEM((STEPS, ROWS, 128), F32),
            pltpu.VMEM((WIDE, 144), BF16),
            pltpu.VMEM(big, BF16),
            pltpu.VMEM(big, BF16),
            pltpu.VMEM((2, 32, WIDE), BF16),
            pltpu.VMEM(big, BF16),
            pltpu.VMEM(big, BF16),
            pltpu.VMEM((WIDE, 96), BF16),
            pltpu.VMEM((2, 32, WIDE), BF16),
            pltpu.VMEM((3, WIDE, 128), F32),
            pltpu.VMEM((WIDE, 96), F32),
            pltpu.VMEM((WIDE, WIDE), F32),
            pltpu.VMEM((WIDE, WIDE), F32),
            pltpu.VMEM((64, WIDE), F32),
            pltpu.VMEM((3, WIDE, 128), F32),
            pltpu.VMEM((STEPS, 2, 4, cols), F32),
            pltpu.VMEM((STEPS, 2, 4, cols), F32),
            pltpu.VMEM((STEPS, 2, 4, cols), F32),
            pltpu.VMEM((STEPS, 2, 4, cols), F32),
            pltpu.VMEM((STEPS, ROWS, 128), F32),
            pltpu.VMEM((STEPS, n, ROWS, 128), F32),
            pltpu.VMEM((HID, 128), F32),
            pltpu.VMEM((n, HID, 128), F32),
            pltpu.SemaphoreType.DMA((2 * STEPS, 2)),
            pltpu.SemaphoreType.DMA((2 * STEPS, 2)),
            pltpu.SemaphoreType.DMA((n,)),
            pltpu.SemaphoreType.DMA((STEPS, n)),
            pltpu.SemaphoreType.DMA((n,)),
            pltpu.SemaphoreType.DMA((n,)),
        ],
        compiler_params=pltpu.CompilerParams(
            collective_id=0, has_side_effects=True, vmem_limit_bytes=56 * 1024 * 1024
        ),
    )(
        state.reshape(4 * ROWS, cols),
        bed_slope.reshape(2 * ROWS, cols),
        terrain,
        wet_mask,
        state_cotangent.reshape(4 * ROWS, cols),
        params,
        roughness,
    )
    feat, outs, layers = first_weight.shape[1], output_weight.shape[0], biases.shape[0]
    return (
        final.reshape(state.shape),
        adjoint.reshape(state.shape),
        grads[:, 0:feat],
        grads[:, 32:64],
        grads[:, 64:96],
        grads[0:outs, 96:128],
        grads[8 : 8 + layers, 96:128],
    )


def solution(mesh):
    cells = P(None, ("grp", "row", "col"), None)
    flat = P(("grp", "row", "col"), None)
    in_specs = (cells, cells, flat, flat, cells, P(), P(), P(), P(), P(), P())
    out_specs = (cells, cells) + (P("grp", None),) * 5
    return jax.shard_map(shards, mesh=mesh, in_specs=in_specs, out_specs=out_specs, check_vma=False)
```

time: 1320 us -> 230 us (0.17)
  matrix products: 536 us -> 0 us
  local copies, waits for them, and re-layouts: 316 us -> 9.71 us
  blocking collectives: 252 us -> 0 us
  Pallas kernels: 0 us -> 219 us
  other arithmetic: 122 us -> 0 us
  starting transfers between devices: 57.8 us -> 0 us
    dot_general x720 -> x0, matrix products: 536 us -> none  [the longest x192 148 us: network(): jnp.dot(first_weight, features, precision=EXACT, preferred_element_type=j...]
    pallas_call x0 -> x1, Pallas kernels: none -> 219 us  [shards(): pl.pallas_call(functools.partial(kernel, n, ncol, cols), out_shape=(jax.S...]
    dynamic_update_slice x192 -> x0, local copies, waits for them, and re-layouts: 197 us -> none  [closure(): lax.map(lambda row_cells: saved(row_cells, *weights), jnp.moveaxis(featur...]
    pmax x6 -> x0, blocking collectives: 192 us -> none  [shards(): deepest = lax.pmax(jnp.max(current[0]), ('row', 'col'))]
    add_any x78 -> x0, other arithmetic: 88.6 us -> none  [the longest x48 50.9 us: closure(): saved(row_cells, *weights)]
    psum x1 -> x0, blocking collectives: 60.1 us -> none  [shards(): lax.psum((partial_grads[0], partial_grads[1], partial_grads[2], partial_g...]
    ppermute x24 -> x0, starting transfers between devices: 57.8 us -> none  [the longest x12 31.5 us: extended(): before = lax.ppermute(last, axis, up)]
    squeeze x48 -> x0, local copies, waits for them, and re-layouts: 49.7 us -> none  [closure(): lax.map(lambda row_cells: saved(row_cells, *weights), jnp.moveaxis(featur...]
  transfers between devices with their start and end apart: 24 -> 0, of which waited for: 6 -> 0; matrix products, arithmetic and copies ran while one was open for 15% -> 0% of each run, Pallas kernels for 0% -> 0%
where the time goes in v1:
time: 230 us; the launch traced here: 229 us
  Pallas kernels  219 us (95%)
  local copies, waits for them, and re-layouts  9.71 us (4%)
    pallas_call x1, Pallas kernels, shards(): pl.pallas_call(functools.partial(kernel, n, ncol, cols), out_shape=(jax.S...  219 us
    unnamed x24, local copies, waits for them, and re-layouts  8.37 us

profile of v1, /device:TPU:0, one launch (start us, length us, event | category | flops | bytes accessed | tf_op | source)
XLA Modules:
  0.0 229.2 jit_solution(12667868244603987347)
XLA Ops:
  0.6 0.0 copy-start.5
  0.6 0.7 copy-done.5
  1.3 0.1 copy.26
  1.4 0.0 copy-start.3
  1.4 0.7 copy-done.3
  2.1 0.0 copy-start.4
  2.1 0.7 copy-done.4
  2.8 0.0 copy-start.6
  2.8 0.7 copy-done.6
  3.5 0.0 copy-start.7
  3.5 0.7 copy-done.7
  4.2 0.0 copy-start.2
  4.2 0.6 copy-done.2
  4.8 218.8 %shard_map.162 = (f32[32,4096]{1,0:T(8,128)}, f32[32,4096]{1,0:T(8,128)}, f32[32,128]{1,0:T(8,128)}) custom-call(f32[32,4096]{1,0:T(8,128)} %bitcast.6, f32[16,4096]{1,0:T(8,128)} %bitcast.10, s32[8,4096]{1,0:T(8,128)} %terrain.1, s32[8,4096]{1,0:T(8,128)} %wet_mask.1, f32[32,4096]{1,0:T(8,128)} %bitcast.7, f32[136,32]{1,0:T(8,128)} %copy-done.2, f32[4]{0:T(128)} %roughness.1), custom_call_target="tpu_custom_call" | custom-call | tf_op jit(solution)/shard_map/pallas_call | solution.py:390
  223.6 0.0 copy-start.1
  223.6 1.4 copy.27
  225.1 0.0 copy-done.1
  225.1 0.7 fusion
  225.7 0.7 fusion.1
  226.4 0.0 copy-start
  226.4 1.9 copy.34
  228.4 0.0 copy-done
  228.4 0.8 copy.35
  (5 shorter events, 0.0 us)
Async XLA Ops:
  0.6 0.7 copy-start.5
  1.4 0.7 copy-start.3
  2.1 0.7 copy-start.4
  2.8 0.7 copy-start.6
  3.5 0.7 copy-start.7
  4.2 0.6 copy-start.2
  223.6 1.5 copy-start.1
  226.4 1.9 copy-start

commit v2 on v1

--- a/solution.py
+++ b/solution.py
@@ -14,8 +14,11 @@
 SMOOTH = 0.2
 HID = 32
 ROWS = 8
-WIDE = HID * ROWS
-CHUNK = 512
+SLOTS = 4
+HALF = HID * SLOTS
+WIDE = 2 * HALF
+CHUNK = 1024
+KEPT = 3
 F32, BF16 = jnp.float32, jnp.bfloat16
 
 
@@ -44,31 +47,42 @@
     return index - period * (index >= period) - period * (index >= 2 * period)
 
 
-def spread(count, period, transposed=False):
-    shape = (HID, count) if transposed else (count, HID)
+def cells(period):
+    def where(i):
+        inner = wrapped(i, period)
+        return inner >> 3, i & 7, (i >= period).astype(jnp.int32) + (i >= 2 * period).astype(jnp.int32)
+
+    return where
+
+
+def units(half_bit=None):
+    def where(i):
+        slot = i & 3
+        if half_bit is not None:
+            slot = slot + 4 * (i >> half_bit)
+        return (i & (HALF - 1)) >> 2, slot, (i >> 7) & 1
+
+    return where
+
+
+def chosen(count, where, transposed=False, lanes=HID, offset=0):
+    shape = (lanes, count) if transposed else (count, lanes)
     stacked, unit = (1, 0) if transposed else (0, 1)
-    return ((wrapped(iota(shape, stacked), period) >> 3) == iota(shape, unit)).astype(F32).astype(BF16)
-
-
-def same_row(shape):
-    return (iota(shape, 0) & 7) == (iota(shape, 1) & 7)
-
-
-def widened(small, rows, cols, transposed, period):
-    keep = same_row((rows, cols))
-    left, right = spread(rows, rows), spread(cols, period)
-    result = []
-    for part in split(small):
-        half = dot(left, part, 1, 1 if transposed else 0).astype(BF16)
-        full = dot(half, right, 1, 1)
-        result.append(jnp.where(keep, full, 0.0))
-    return result
-
-
-def stacked3(small, rows, unit, transposed):
-    hi, lo = widened(small, rows, 3 * unit, transposed, unit)
-    col = iota(hi.shape, 1)
-    return jnp.where((col >= unit) & (col < 2 * unit), lo, hi).astype(BF16)
+    return (where(iota(shape, stacked))[0] + offset == iota(shape, unit)).astype(F32).astype(BF16)
+
+
+def same_row(shape, row_where, col_where):
+    return row_where(iota(shape, 0))[1] == col_where(iota(shape, 1))[1]
+
+
+def widened(small, shape, row_where, col_where, is_low, transposed):
+    left, right = chosen(shape[0], row_where), chosen(shape[1], col_where)
+    hi, lo = (
+        dot(dot(left, part, 1, 1 if transposed else 0).astype(BF16), right, 1, 1) for part in split(small)
+    )
+    low = is_low(row_where(iota(shape, 0))[2], col_where(iota(shape, 1))[2])
+    full = jnp.where(low, lo, hi)
+    return jnp.where(same_row(shape, row_where, col_where), full, 0.0).astype(BF16)
 
 
 def shifted(x, before, after):
@@ -86,7 +100,7 @@
     state, bed, terrain, wet_mask, cotangent, params, roughness,
     final, adjoint, grads,
     traj, lam, drag, dfeat, rough_wet, wet, steps_dt,
-    w1, w2, w3, w4, w2t, w3t, w4t, w1t, bias,
+    w1, w2, w3, w4, w2t, w3t, w4t, w1t, bias, kept,
     g1, g2, g3, g4, gb,
     edge_f, halo_f, edge_b, halo_b, peak, peaks, own_grad, all_grads,
     edge_ss, edge_rs, peak_ss, peak_rs, grad_ss, grad_rs,
@@ -107,17 +121,17 @@
         pl.semaphore_signal(barrier, inc=1, device_id=device(peer(i)), device_id_type=pl.DeviceIdType.MESH)
 
     m1, m2, m3, m4 = (params[32 * i : 32 * i + 32, :] for i in range(4))
-    w1[...] = stacked3(m1, WIDE, 48, False)
-    w4t[...] = stacked3(m4, WIDE, 32, True)
-    for ref, small, rows, transposed in (
-        (w2, m2, WIDE, False), (w3, m3, WIDE, False), (w4, m4, 32, False),
-        (w2t, m2, WIDE, True), (w3t, m3, WIDE, True), (w1t, m1, 32, True),
-    ):
-        for k, part in enumerate(widened(small, rows, WIDE, transposed, WIDE)):
-            ref[k] = part.astype(BF16)
+    low_col = lambda r, c: c == 1
+    low_row = lambda r, c: r == 1
+    w1[...] = widened(m1, (WIDE, 144), units(7), cells(48), low_col, False)
+    w4t[...] = widened(m4, (WIDE, 96), units(7), cells(32), low_col, True)
+    w4[...] = widened(m4, (64, 2 * WIDE), cells(32), units(8), low_row, False)
+    w1t[...] = widened(m1, (64, 2 * WIDE), cells(32), units(8), low_row, True)
+    for ref, small, transposed in ((w2, m2, False), (w3, m3, False), (w2t, m2, True), (w3t, m3, True)):
+        ref[...] = widened(small, (WIDE, WIDE), units(), units(), low_row, transposed)
     for layer in range(3):
         line = jnp.broadcast_to(params[128 + layer : 129 + layer, :], (128, HID))
-        bias[layer] = sum(dot(spread(WIDE, WIDE), part, 1, 1) for part in split3(line))
+        bias[layer] = sum(dot(chosen(HALF, units()), part, 1, 1) for part in split3(line))
     for ref in (g1, g2, g3, g4, gb):
         ref[...] = jnp.zeros_like(ref)
     kinds = terrain[...]
@@ -184,20 +198,39 @@
     def across(tile, width):
         return jnp.concatenate([tile] * (width // 128), axis=1)
 
-    def layer(weight, hi, lo):
-        return dot(weight[0], hi) + dot(weight[0], lo) + dot(weight[1], hi)
-
-    def hidden(step, at):
-        x = jnp.concatenate([traj[step, :, at], bed[:, at]], axis=0)
-        xhi, xlo = split(x)
-        a1 = jnp.tanh(dot(w1[...], jnp.concatenate([xhi, xhi, xlo], axis=0)) + across(bias[0], CHUNK))
-        s1 = split(a1)
-        a2 = jnp.tanh(layer(w2, *s1) + across(bias[1], CHUNK))
-        s2 = split(a2)
-        a3 = jnp.tanh(layer(w3, *s2) + across(bias[2], CHUNK))
-        return (xhi, xlo), a1, s1, a2, s2, a3, split(a3)
-
-    def forward(step, _):
+    def folded(y):
+        half = y.shape[0] // 2
+        return y[:half] + y[half:]
+
+    def side(y):
+        return jnp.concatenate([y[:HALF], y[HALF:]], axis=1)
+
+    def under(y):
+        return jnp.concatenate([y[:, :CHUNK], y[:, CHUNK:]], axis=0)
+
+    def pair(x):
+        return jnp.concatenate(split(x), axis=0)
+
+    def features(step, at):
+        return split(jnp.concatenate([traj[step, :, at], bed[:, at]], axis=0))
+
+    def hidden(xhi, xlo):
+        wide = 2 * CHUNK
+        a1 = jnp.tanh(side(dot(w1[...], jnp.concatenate([xhi, xhi, xlo], axis=0))) + across(bias[0], wide))
+        s1 = pair(a1)
+        a2 = jnp.tanh(folded(dot(w2[...], s1)) + across(bias[1], wide))
+        s2 = pair(a2)
+        a3 = jnp.tanh(folded(dot(w3[...], s2)) + across(bias[2], wide))
+        return a1, s1, a2, s2, a3, pair(a3)
+
+    def recalled(step, c):
+        result = []
+        for k in range(3):
+            both = kept[step, c, k]
+            result += [both[:HALF].astype(F32) + both[HALF:].astype(F32), both]
+        return result
+
+    def forward(keep, step, _):
         send_edges(step, step, edge_f, halo_f, lambda f, r: traj[step, 8 * f + r : 8 * f + r + 1, :])
         depth = traj[step, 0:ROWS, :]
         deepest = depth[:, 0:128]
@@ -213,8 +246,11 @@
         @pl.loop(0, cols // CHUNK)
         def _(c):
             at = pl.ds(pl.multiple_of(c * CHUNK, CHUNK), CHUNK)
-            s3 = hidden(step, at)[-1]
-            drag[:, at] = layer(w4, *s3)
+            _, s1, _, s2, _, s3 = hidden(*features(step, at))
+            if keep:
+                for k, both in enumerate((s1, s2, s3)):
+                    kept[step, c, k] = both
+            drag[:, at] = folded(dot(w4[...], under(s3)))
 
         @pl.loop(1, n)
         def _(i):
@@ -254,10 +290,11 @@
         traj[step + 1, 24:32, :] = fields[3] + smooth[3] + dt * wet[...] * drag[16:24, :]
         return 0
 
-    lax.fori_loop(0, STEPS, forward, 0)
+    lax.fori_loop(0, KEPT, functools.partial(forward, True), 0)
+    lax.fori_loop(KEPT, STEPS, functools.partial(forward, False), 0)
     final[...] = traj[STEPS]
 
-    def backward(back, _):
+    def backward(keep, back, _):
         step = STEPS - 1 - back
         number = STEPS + step
         send_edges(number, step, edge_b, halo_b, lambda f, r: lam[8 * f + r : 8 * f + r + 1, :])
@@ -273,23 +310,22 @@
                 axis=0,
             )
             ghi, glo = split(g)
-            (xhi, xlo), a1, s1, a2, s2, a3, s3 = hidden(step, at)
-            d3 = dot(w4t[...], jnp.concatenate([ghi, ghi, glo], axis=0)) * (1.0 - a3 * a3)
-            t3 = split(d3)
-            d2 = layer(w3t, *t3) * (1.0 - a2 * a2)
-            t2 = split(d2)
-            d1 = layer(w2t, *t2) * (1.0 - a1 * a1)
-            t1 = split(d1)
-            dfeat[:, at] = layer(w1t, *t1)
-            both_g = jnp.concatenate([ghi, glo], axis=0)
-            both_x = jnp.concatenate([xhi, xlo], axis=0)
-            g4[...] += dot(both_g, s3[0], 1, 1) + dot(both_g, s3[1], 1, 1)
-            g3[...] += dot(t3[0], s2[0], 1, 1) + dot(t3[0], s2[1], 1, 1) + dot(t3[1], s2[0], 1, 1)
-            g2[...] += dot(t2[0], s1[0], 1, 1) + dot(t2[0], s1[1], 1, 1) + dot(t2[1], s1[0], 1, 1)
-            g1[...] += dot(t1[0], both_x, 1, 1) + dot(t1[1], both_x, 1, 1)
+            xhi, xlo = features(step, at)
+            a1, s1, a2, s2, a3, s3 = recalled(step, c) if keep else hidden(xhi, xlo)
+            d3 = side(dot(w4t[...], jnp.concatenate([ghi, ghi, glo], axis=0))) * (1.0 - a3 * a3)
+            t3 = pair(d3)
+            d2 = folded(dot(w3t[...], t3)) * (1.0 - a2 * a2)
+            t2 = pair(d2)
+            d1 = folded(dot(w2t[...], t2)) * (1.0 - a1 * a1)
+            t1 = under(pair(d1))
+            dfeat[:, at] = folded(dot(w1t[...], t1))
+            g4[...] += dot(jnp.concatenate([ghi, glo], axis=0), under(s3), 1, 1)
+            g3[...] += dot(t3, s2, 1, 1)
+            g2[...] += dot(t2, s1, 1, 1)
+            g1[...] += dot(t1, jnp.concatenate([xhi, xlo], axis=0), 1, 1)
             for k, d in enumerate((d1, d2, d3)):
                 total = d[:, 0:128]
-                for j in range(1, CHUNK // 128):
+                for j in range(1, 2 * CHUNK // 128):
                     total = total + d[:, 128 * j : 128 * j + 128]
                 gb[k] += total
 
@@ -315,29 +351,26 @@
         lam[24:32, :] = lams[3] + smooth[3] + dfeat[24:32, :]
         return 0
 
-    lax.fori_loop(0, STEPS, backward, 0)
+    lax.fori_loop(0, STEPS - KEPT, functools.partial(backward, False), 0)
+    lax.fori_loop(STEPS - KEPT, STEPS, functools.partial(backward, True), 0)
     adjoint[...] = lam[...]
 
-    def place(count, period, offset):
-        shape = (count, 128)
-        return ((wrapped(iota(shape, 0), period) >> 3) + offset == iota(shape, 1)).astype(F32).astype(BF16)
-
-    def collapsed(total, period, col_period, offset):
-        rows, width = total.shape
-        total = jnp.where(same_row(total.shape), total, 0.0)
-        gather = spread(rows, period, transposed=True)
+    def collapsed(total, row_where, col_where, offset):
+        total = jnp.where(same_row(total.shape, row_where, col_where), total, 0.0)
+        gather = chosen(total.shape[0], row_where, transposed=True)
+        put = chosen(total.shape[1], col_where, lanes=128, offset=offset)
         half = sum(dot(gather, part) for part in split3(total))
-        put = place(width, col_period, offset)
         return sum(dot(part, put) for part in split3(half))
 
-    packed = collapsed(g1[...], WIDE, 48, 0)
-    packed += collapsed(g2[...], WIDE, WIDE, 32)
-    packed += collapsed(g3[...], WIDE, WIDE, 64)
-    packed += collapsed(g4[...], 32, WIDE, 96)
+    packed = collapsed(g1[...], units(8), cells(48), 0)
+    packed += collapsed(g2[...], units(), units(), 32)
+    packed += collapsed(g3[...], units(), units(), 64)
+    packed += collapsed(g4[...], cells(32), units(8), 96)
     for k in range(3):
         pick = (iota((HID, 128), 0) == 8 + k).astype(F32).astype(BF16)
         half = sum(dot(pick, part, 1, 1) for part in split3(gb[k]))
-        packed += sum(dot(part, place(WIDE, WIDE, 96)) for part in split3(half))
+        put = chosen(HALF, units(), lanes=128, offset=96)
+        packed += sum(dot(part, put) for part in split3(half))
     own_grad[...] = packed
     all_grads[me] = packed
 
@@ -386,7 +419,7 @@
         axis=0,
     )
     vmem = pl.BlockSpec(memory_space=pltpu.VMEM)
-    big = (2, WIDE, WIDE)
+    big = (WIDE, WIDE)
     final, adjoint, grads = pl.pallas_call(
         functools.partial(kernel, n, ncol, cols),
         out_shape=(
@@ -407,17 +440,18 @@
             pltpu.VMEM((WIDE, 144), BF16),
             pltpu.VMEM(big, BF16),
             pltpu.VMEM(big, BF16),
-            pltpu.VMEM((2, 32, WIDE), BF16),
+            pltpu.VMEM((64, 2 * WIDE), BF16),
             pltpu.VMEM(big, BF16),
             pltpu.VMEM(big, BF16),
             pltpu.VMEM((WIDE, 96), BF16),
-            pltpu.VMEM((2, 32, WIDE), BF16),
-            pltpu.VMEM((3, WIDE, 128), F32),
-            pltpu.VMEM((WIDE, 96), F32),
+            pltpu.VMEM((64, 2 * WIDE), BF16),
+            pltpu.VMEM((3, HALF, 128), F32),
+            pltpu.VMEM((KEPT, cols // CHUNK, 3, WIDE, 2 * CHUNK), BF16),
+            pltpu.VMEM((2 * WIDE, 96), F32),
             pltpu.VMEM((WIDE, WIDE), F32),
             pltpu.VMEM((WIDE, WIDE), F32),
-            pltpu.VMEM((64, WIDE), F32),
-            pltpu.VMEM((3, WIDE, 128), F32),
+            pltpu.VMEM((64, 2 * WIDE), F32),
+            pltpu.VMEM((3, HALF, 128), F32),
             pltpu.VMEM((STEPS, 2, 4, cols), F32),
             pltpu.VMEM((STEPS, 2, 4, cols), F32),
             pltpu.VMEM((STEPS, 2, 4, cols), F32),
@@ -434,7 +468,7 @@
             pltpu.SemaphoreType.DMA((n,)),
         ],
         compiler_params=pltpu.CompilerParams(
-            collective_id=0, has_side_effects=True, vmem_limit_bytes=56 * 1024 * 1024
+            collective_id=0, has_side_effects=True, vmem_limit_bytes=62 * 1024 * 1024
         ),
     )(
         state.reshape(4 * ROWS, cols),
@@ -458,8 +492,8 @@
 
 
 def solution(mesh):
-    cells = P(None, ("grp", "row", "col"), None)
+    grid = P(None, ("grp", "row", "col"), None)
     flat = P(("grp", "row", "col"), None)
-    in_specs = (cells, cells, flat, flat, cells, P(), P(), P(), P(), P(), P())
-    out_specs = (cells, cells) + (P("grp", None),) * 5
+    in_specs = (grid, grid, flat, flat, grid, P(), P(), P(), P(), P(), P())
+    out_specs = (grid, grid) + (P("grp", None),) * 5
     return jax.shard_map(shards, mesh=mesh, in_specs=in_specs, out_specs=out_specs, check_vma=False)

time: 230 us -> 136 us (0.59)
  Pallas kernels: 219 us -> 125 us
    pallas_call x1, Pallas kernels: 219 us -> 125 us  [shards(): pl.pallas_call(functools.partial(kernel, n, ncol, cols), out_shape=(jax.S...]
where the time goes in v2:
time: 136 us
  Pallas kernels  125 us (92%)
  local copies, waits for them, and re-layouts  9.71 us (7%)
    pallas_call x1, Pallas kernels, shards(): pl.pallas_call(functools.partial(kernel, n, ncol, cols), out_shape=(jax.S...  125 us
    unnamed x24, local copies, waits for them, and re-layouts  8.37 us

profile of v2, /device:TPU:0, one launch (start us, length us, event | category | flops | bytes accessed | tf_op | source)
XLA Modules:
  0.0 135.5 jit_solution(11176076440708350561)
XLA Ops:
  0.6 0.0 copy-start.5
  0.6 0.7 copy-done.5
  1.3 0.1 copy.26
  1.4 0.0 copy-start.3
  1.4 0.7 copy-done.3
  2.1 0.0 copy-start.4
  2.1 0.7 copy-done.4
  2.8 0.0 copy-start.6
  2.8 0.7 copy-done.6
  3.5 0.0 copy-start.7
  3.5 0.7 copy-done.7
  4.2 0.0 copy-start.2
  4.2 0.6 copy-done.2
  4.8 125.1 %shard_map.162 = (f32[32,4096]{1,0:T(8,128)}, f32[32,4096]{1,0:T(8,128)}, f32[32,128]{1,0:T(8,128)}) custom-call(f32[32,4096]{1,0:T(8,128)} %bitcast.6, f32[16,4096]{1,0:T(8,128)} %bitcast.10, s32[8,4096]{1,0:T(8,128)} %terrain.1, s32[8,4096]{1,0:T(8,128)} %wet_mask.1, f32[32,4096]{1,0:T(8,128)} %bitcast.7, f32[136,32]{1,0:T(8,128)} %copy-done.2, f32[4]{0:T(128)} %roughness.1), custom_call_target="tpu_custom_call" | custom-call | tf_op jit(solution)/shard_map/pallas_call | solution.py:423
  130.0 0.0 copy-start.1
  130.0 1.4 %copy.27 = f32[32,6]{0,1:T(8,128)} copy(f32[32,6]{1,0:T(8,128)} %bitcast.11) | data formatting | bytes 1536
  131.5 0.0 copy-done.1
  131.5 0.7 fusion
  132.1 0.7 fusion.1
  132.8 0.0 copy-start
  132.8 1.9 %copy.34 = f32[4,8,4096]{2,1,0:T(8,128)} copy(f32[4,8,4096]{2,1,0:T(8,128)} %bitcast.9) | data formatting | bytes 1048576
  134.7 0.0 copy-done
  134.7 0.8 copy.35
  (5 shorter events, 0.0 us)
Async XLA Ops:
  0.6 0.7 copy-start.5
  1.4 0.7 copy-start.3
  2.1 0.7 copy-start.4
  2.8 0.7 copy-start.6
  3.5 0.7 copy-start.7
  4.2 0.6 copy-start.2
  130.0 1.5 %copy-start.1 = (f32[32,128]{1,0:T(8,128)S(1)}, f32[32,128]{1,0:T(8,128)}, u32[]{:S(2)}) copy-start(f32[32,128]{1,0:T(8,128)} %get-tuple-element.12) | copy-start | bytes 49156
  132.8 1.9 %copy-start = (f32[32,4096]{1,0:T(8,128)S(1)}, f32[32,4096]{1,0:T(8,128)}, u32[]{:S(2)}) copy-start(f32[32,4096]{1,0:T(8,128)} %get-tuple-element.11) | copy-start | bytes 1572868
